TPU v7x, 128 devices: a whole 4x4x4 slice. The times are simulated.
128 devices in a mesh: dom: 4 (over x), head: 32 (over z, y, core).
Axes of the slice: x: 4, y: 4, z: 4, core: 2. Of those that a mesh axis runs over, the one named last changes fastest.
Arguments:
- tokens: bfloat16 [24, 64, 8192], P(None, 'dom', 'head'), may hold values from -6 to 6
- parents: int32 [64], replicated, may hold values from 0 to 63, as said below
- recurrent_state: float32 [64, 128, 64, 256], P('dom', 'head'), may hold values from -6 to 6
- value_history: float32 [64, 3, 8192], P('dom', None, 'head'), may hold values from -6 to 6
- mixing_history: float32 [64, 3, 2048], P('dom', None, 'head'), may hold values from -6 to 6
- input_gain: float32 [8192], P('head'), may hold values from 0.5 to 1.5
- gate_value_weight: bfloat16 [8192, 2, 8192], P(None, None, 'head'), may hold values from -0.0625 to 0.0625
- mixing_weight: bfloat16 [8192, 2048], P(None, 'head'), may hold values from -0.0625 to 0.0625
- step_weight: bfloat16 [8192, 128], P(None, 'head'), may hold values from -0.0625 to 0.0625
- value_kernel: float32 [4, 8192], P(None, 'head'), may hold values from -3 to 3
- value_offset: float32 [8192], P('head'), may hold values from -0.5 to 0.5
- mixing_kernel: float32 [4, 2048], P(None, 'head'), may hold values from -3 to 3
- mixing_offset: float32 [2048], P('head'), may hold values from -0.5 to 0.5
- step_offset: float32 [128], P('head'), may hold values from -4 to 0
- decay_log: float32 [128], P('head'), may hold values from -2 to 1.5
- skip_gain: float32 [128], P('head'), may hold values from 0.5 to 1.5
- output_gain: float32 [8192], P('head'), may hold values from 0.5 to 1.5
- output_weight: bfloat16 [8192, 8192], P('head'), may hold values from -0.0625 to 0.0625
Outputs:
- mixed: bfloat16 [24, 64, 8192], P(None, 'dom', 'head')
Inputs may be any that keep to these rules, and one draw needn't show every extreme that they name: parents comes from systematic resampling: it never falls with i, and offspring counts are very uneven, so that a particle's parent may sit several blocks of 16 particles away.
All inputs are finite; a program needn't handle non-finite values.
Results may differ from a plain program's by a relative error of at most 0.023.
Values may be sent and summed in bfloat16 or wider, within the bound.
A program may use at most 128 MiB of HBM per device.

v0:
```python
import jax
import jax.numpy as jnp
from jax import lax
from jax.sharding import PartitionSpec as P

HEADS = 128
GROUPS = 4
P_SIZE = 64


def causal_conv(previous, current, kernel, shift_bias):
    window = jnp.concatenate([jnp.moveaxis(previous, 1, 0), current], axis=0)
    length = current.shape[0]
    summed = jnp.zeros_like(current)
    for tap_index in range(kernel.shape[0]):
        summed = summed + kernel[tap_index] * window[tap_index : tap_index + length]
    return jax.nn.silu(summed + shift_bias)


def pick_rows(carried, pieces, wanted):
    counted = pieces[0].shape[0]
    inside = (wanted >= 0) & (wanted < counted)
    safe_rows = jnp.clip(wanted, 0, counted - 1)
    result = []
    for held_rows, source in zip(carried, pieces):
        taken_rows = jnp.take(source, safe_rows, axis=0)
        mask_shape = (wanted.shape[0],) + (1,) * (source.ndim - 1)
        result.append(jnp.where(inside.reshape(mask_shape), taken_rows, held_rows))
    return tuple(result)


def body(
    tokens,
    parents,
    recurrent_state,
    value_history,
    mixing_history,
    input_gain,
    gate_value_weight,
    mixing_weight,
    step_weight,
    value_kernel,
    value_offset,
    mixing_kernel,
    mixing_offset,
    step_offset,
    decay_log,
    skip_gain,
    output_gain,
    output_weight,
):
    steps_count, local_particles, local_width = tokens.shape
    local_heads, head_width, state_width = (
        recurrent_state.shape[1],
        recurrent_state.shape[2],
        recurrent_state.shape[3],
    )
    channels = local_heads * head_width
    row_count = steps_count * local_particles
    dom_index = lax.axis_index("dom")
    head_count = lax.axis_size("head")
    head_index = lax.axis_index("head")
    gathered, full_gain = (
        lax.all_gather(tokens, "head", axis=2, tiled=True),
        lax.all_gather(input_gain.astype(jnp.bfloat16), "head", axis=0, tiled=True).astype(
            input_gain.dtype
        ),
    )
    flat_tokens = gathered.astype(jnp.float32).reshape(row_count, -1)
    normed = (
        flat_tokens
        * lax.rsqrt(jnp.mean(flat_tokens * flat_tokens, axis=-1, keepdims=True) + 1e-05)
        * full_gain
    ).astype(jnp.bfloat16)
    gate_value = jnp.dot(
        normed,
        gate_value_weight.reshape(gate_value_weight.shape[0], 2 * channels),
        preferred_element_type=jnp.float32,
    ).reshape(steps_count, local_particles, 2, channels)
    mixing_raw = jnp.dot(normed, mixing_weight, preferred_element_type=jnp.float32).reshape(
        steps_count, local_particles, -1
    )
    step_raw = jnp.dot(normed, step_weight, preferred_element_type=jnp.float32).reshape(
        steps_count, local_particles, local_heads
    )
    first_child = dom_index * local_particles
    own_parents = lax.dynamic_slice_in_dim(parents, first_child, local_particles)
    initial = (
        jnp.zeros_like(recurrent_state),
        jnp.zeros_like(value_history),
        jnp.zeros_like(mixing_history),
    )
    start_state, value_prev, mixing_prev = pick_rows(
        initial,
        (
            lax.all_gather(recurrent_state.astype(jnp.bfloat16), "dom", axis=0, tiled=True).astype(
                jnp.float32
            ),
            lax.all_gather(value_history.astype(jnp.bfloat16), "dom", axis=0, tiled=True).astype(
                jnp.float32
            ),
            lax.all_gather(mixing_history.astype(jnp.bfloat16), "dom", axis=0, tiled=True).astype(
                jnp.float32
            ),
        ),
        own_parents,
    )
    value_act = causal_conv(value_prev, gate_value[:, :, 1], value_kernel, value_offset).reshape(
        steps_count, local_particles, local_heads, head_width
    )
    mixing_act = causal_conv(mixing_prev, mixing_raw, mixing_kernel, mixing_offset)
    mixing_all = lax.all_gather(mixing_act.astype(jnp.bfloat16), "head", axis=2, tiled=True).astype(
        mixing_act.dtype
    )
    per_group = head_count // GROUPS
    group_index = head_index // per_group
    input_mix = lax.dynamic_slice_in_dim(mixing_all, group_index * state_width, state_width, 2)
    output_mix = lax.dynamic_slice_in_dim(
        mixing_all, (GROUPS + group_index) * state_width, state_width, 2
    )
    step_size = jax.nn.softplus(step_raw + step_offset)
    decay = jnp.exp(-step_size * jnp.exp(decay_log))
    skip_term = skip_gain[:, None] * value_act

    def advance(state_now, inputs):
        value_now, input_now, output_now, size_now, decay_now = inputs
        state_now = (
            decay_now[:, :, None, None] * state_now
            + (size_now[:, :, None] * value_now)[..., None] * input_now[:, None, None, :]
        )
        read_out = jnp.einsum(
            "bhpn,bn->bhp", state_now, output_now, precision=lax.Precision.HIGHEST
        )
        return (state_now, read_out)

    unused_state, local_read = lax.scan(
        advance, start_state, (value_act, input_mix, output_mix, step_size, decay)
    )
    read_all = local_read + skip_term
    gated = read_all * jax.nn.silu(
        gate_value[:, :, 0].reshape(steps_count, local_particles, local_heads, head_width)
    )
    squares = jnp.sum(gated * gated, axis=(2, 3))
    selector = jnp.arange(GROUPS, dtype=jnp.int32) == group_index
    slots = jnp.where(selector, squares[..., None], 0.0)
    summed = lax.psum(slots, "head")
    group_total = jnp.sum(jnp.where(selector, summed, 0.0), axis=-1)
    square_mean = group_total / (HEADS // GROUPS * P_SIZE)
    scaled = (
        (gated * lax.rsqrt(square_mean[..., None, None] + 1e-05)).reshape(row_count, channels)
        * output_gain
    ).astype(jnp.bfloat16)
    output_terms = jnp.dot(scaled, output_weight, preferred_element_type=jnp.float32).reshape(
        steps_count, local_particles, -1
    )
    return lax.psum_scatter(
        output_terms.astype(jnp.bfloat16), "head", scatter_dimension=2, tiled=True
    )


def solution(mesh):
    return jax.shard_map(
        body,
        mesh=mesh,
        in_specs=(
            P(None, "dom", "head"),
            P(),
            P("dom", "head", None, None),
            P("dom", None, "head"),
            P("dom", None, "head"),
            P("head"),
            P(None, None, "head"),
            P(None, "head"),
            P(None, "head"),
            P(None, "head"),
            P("head"),
            P(None, "head"),
            P("head"),
            P("head"),
            P("head"),
            P("head"),
            P("head"),
            P("head", None),
        ),
        out_specs=P(None, "dom", "head"),
        check_vma=False,
    )
```

profile of v0, /device:TPU:0, one launch (start us, length us, event | category | flops | bytes accessed | tf_op | source)
XLA Modules:
  0.0 750.3 jit_solution(15983251670227247696)
XLA Ops:
  11.3 8.1 %copy.52 = bf16[1024,8,2,256]{3,1,2,0:T(8,128)(2,1)} copy(bf16[1024,8,2,256]{3,2,1,0:T(2,128)(2,1)} %bitcast.78) | data formatting | bytes 16777216
  19.4 11.5 %copy.43 = bf16[512,8192]{1,0:T(8,128)(2,1)} copy(bf16[512,8192]{0,1:T(8,128)(2,1)} %bitcast.77) | data formatting | bytes 16777216 | tf_op jit(solution)/shard_map/dot_general | solution.py:75
  30.9 25.8 %all-gather = bf16[32,1,256]{2,1,0:T(2,128)(2,1)S(1)} all-gather(bf16[1,1,256]{2,1,0:T(2,128)(2,1)S(1)} %reshape.138), channel_id=1, replica_groups=mesh['dom'=4,'head'=32] {'head'}, dimensions={0}, use_global_device_ids=true | all-gather | bytes 16896 | tf_op jit(solution)/shard_map/all_gather | solution.py:65
  56.8 12.3 %all_gather.21 = bf16[64,3,256]{2,0,1:T(8,128)(2,1)S(1)} all-gather(bf16[16,3,256]{2,0,1:T(8,128)(2,1)S(1)} %convert_element_type.52), channel_id=1, replica_groups=mesh['dom'=4,'head'=32] {'dom'}, dimensions={0}, use_global_device_ids=true | all-gather | bytes 122880 | tf_op jit(solution)/shard_map/all_gather | solution.py:99
  69.2 11.9 %all_gather.22 = bf16[64,3,64]{2,0,1:T(8,128)(2,1)S(1)} all-gather(bf16[16,3,64]{2,0,1:T(8,128)(2,1)S(1)} %convert_element_type.54), channel_id=1, replica_groups=mesh['dom'=4,'head'=32] {'dom'}, dimensions={0}, use_global_device_ids=true | all-gather | bytes 30720 | tf_op jit(solution)/shard_map/all_gather | solution.py:102
  90.7 7.9 %fusion.5 = f32[24,16,2,256]{3,1,2,0:T(8,128)S(1)} fusion(bf16[2,256,8192,1]{2,1,0,3:T(8,128)(2,1)} %bitcast.79, bf16[24,16,8192]{2,1,0:T(8,128)(2,1)} %all-gather.7.cloned.1.call-done, f32[8192]{0:T(1024)S(1)} %bitcast.82, f32[24,16]{1,0:T(8,128)S(1)} %add_rsqrt_fusion.1), kind=kOutput, calls=%fused_computation.18 | convolution fusion | flops 3233808384 | bytes 15500800 | tf_op jit(solution)/shard_map/dot_general | solution.py:75
  100.4 10.4 %multiply_exponential_fusion = (f32[24,16,4]{1,2,0:T(4,128)S(1)}, f32[24,16,4]{1,2,0:T(4,128)S(1)}) fusion(f32[4]{0:T(128)S(1)} %exp.23, f32[4]{0:T(128)S(1)} %copy-done.16, bf16[8192,4]{0,1:T(4,128)(2,1)S(1)} %copy-done.13, bf16[24,16,8192]{2,1,0:T(8,128)(2,1)} %all-gather.7.cloned.1.call-done, f32[8192]{0:T(1024)S(1)} %bitcast.83, ...), kind=kOutput, calls=%fused_computation.69 | convolution fusion | flops 37762560 | bytes 6403616 | tf_op jit(solution)/shard_map/dot_general | solution.py:83
  110.8 40.1 %all-gather.5.cloned.1.call-done = bf16[64,4,64,256]{3,2,1,0:T(8,128)(2,1)} async-done(((bf16[16,4,64,256]{3,2,1,0:T(8,128)(2,1)}), bf16[64,4,64,256]{3,2,1,0:T(8,128)(2,1)}) %all-gather.5.cloned.1.call-update) | async-done | bytes 8388624 | tf_op jit(solution)/shard_map/all_gather | solution.py:96
  150.9 11.3 %convert_element_type.47 = f32[64,4,64,256]{3,2,1,0:T(8,128)} convert(bf16[64,4,64,256]{3,2,1,0:T(8,128)(2,1)} %all-gather.5.cloned.1.call-done) | non-fusion elementwise | flops 4194304 | bytes 25165824 | tf_op jit(solution)/shard_map/convert_element_type | solution.py:96
  162.2 8.9 %gather_fusion = f32[16,4,64,256]{3,2,1,0:T(8,128)} fusion(f32[64,4,64,256]{3,2,1,0:T(8,128)} %convert_element_type.47, s32[1024]{0:T(1024)S(1)} %pad_clamp_fusion), kind=kCustom, calls=%fused_computation | custom fusion | bytes 8388672 | tf_op jit(solution)/shard_map/jit(_take)/gather | solution.py:26
  176.3 30.9 %all-gather.9.cloned.1.call-done = bf16[24,16,2048]{0,1,2:T(8,128)(2,1)} async-done(((bf16[24,16,64]{0,1,2:T(8,128)(2,1)}), bf16[24,16,2048]{0,1,2:T(8,128)(2,1)}) %all-gather.9.cloned.1.call-update) | async-done | bytes 1572880 | tf_op jit(solution)/shard_map/all_gather | solution.py:112
  218.0 306.0 %while.12 = (s32[]{:T(128)}, f32[16,4,64,256]{3,2,1,0:T(8,128)}, f32[24,16,4,64]{3,2,1,0:T(4,128)}, f32[24,16,4]{1,2,0:T(4,128)S(1)}, f32[24,16,4]{1,2,0:T(4,128...) while((s32[]{:T(128)}, f32[16,4,64,256]{3,2,1,0:T(8,128)}, ...), condition=%wide.region_2.3_spmd, body=%wide.region_1.2_spmd.sunk | while | flops 15732738 | bytes 12798585 | solution.py:136
  223.0 7.2 fusion.55
  235.7 7.2 fusion.55
  248.5 7.2 fusion.55
  261.2 7.2 fusion.55
  274.0 7.2 fusion.55
  286.7 7.2 fusion.55
  299.5 7.2 fusion.55
  376.0 7.2 fusion.55
  414.2 7.2 fusion.55
  439.7 7.2 fusion.55
  526.6 126.5 %psum.7 = f32[24,16,4]{1,2,0:T(4,128)S(1)} all-reduce(f32[24,16,4]{1,2,0:T(4,128)S(1)} %broadcast_select_fusion), channel_id=1, replica_groups=mesh['dom'=4,'head'=32] {'head'}, use_global_device_ids=true, to_apply=%region_4.5 | all-reduce | flops 1536 | bytes 12288 | tf_op jit(solution)/shard_map/psum | solution.py:146
  661.0 82.8 %reduce-scatter.2.cloned.1.call-done = bf16[24,16,256]{2,1,0:T(8,128)(2,1)} async-done(((bf16[24,16,8192]{2,1,0:T(8,128)(2,1)}), bf16[24,16,256]{2,1,0:T(8,128)(2,1)}) %reduce-scatter.2.cloned.1.call-update) | async-done | bytes 196624 | tf_op jit(solution)/shard_map/reduce_scatter | solution.py:156
  (289 shorter events, 276.6 us)
Async XLA Ops:
  6.5 80.5 %copy-start = (bf16[8192,64]{0,1:T(8,128)(2,1)S(1)}, bf16[8192,64]{0,1:T(8,128)(2,1)}, u32[]{:S(2)}) copy-start(bf16[8192,64]{0,1:T(8,128)(2,1)} %param.27) | copy-start | bytes 3145732
  6.5 76.1 %all-gather.7.cloned.1.call-start = ((), (), s32[]{:S(2)}) async-start(), calls=%async_computation.2 | async-start | bytes 6488064 | tf_op jit(solution)/shard_map/all_gather | solution.py:64
  7.3 143.7 %all-gather.5.cloned.1.call-start = ((), (), s32[]{:S(2)}) async-start(), calls=%async_computation.1 | async-start | bytes 10485760 | tf_op jit(solution)/shard_map/all_gather | solution.py:96
  11.2 196.0 %all-gather.9.cloned.1.call-start = ((), (), s32[]{:S(2)}) async-start(), calls=%async_computation.3 | async-start | bytes 8650752 | tf_op jit(solution)/shard_map/all_gather | solution.py:112
  19.4 11.5 %copy-start.14 = (f32[256]{0:T(256)S(1)}, f32[256]{0:T(256)}, u32[]{:S(2)}) copy-start(f32[256]{0:T(256)} %param.25) | copy-start | bytes 3076
  19.4 37.4 %copy-start.15 = (f32[4]{0:T(128)S(1)}, f32[4]{0:T(128)}, u32[]{:S(2)}) copy-start(f32[4]{0:T(128)} %param.34) | copy-start | bytes 52
  19.4 37.4 %copy-start.4 = (f32[16,3,256]{2,0,1:T(8,128)S(1)}, f32[16,3,256]{2,0,1:T(8,128)}, u32[]{:S(2)}) copy-start(f32[16,3,256]{2,0,1:T(8,128)} %param.23) | copy-start | bytes 147460
  19.4 49.8 %copy-start.5 = (f32[16,3,64]{2,0,1:T(8,128)S(1)}, f32[16,3,64]{2,0,1:T(8,128)}, u32[]{:S(2)}) copy-start(f32[16,3,64]{2,0,1:T(8,128)} %param.24) | copy-start | bytes 36868
  19.4 61.8 %copy-start.11 = (s32[64]{0:T(128)S(1)}, s32[64]{0:T(128)}, u32[]{:S(2)}) copy-start(s32[64]{0:T(128)} %param.21) | copy-start | bytes 772
  19.4 63.1 %copy-start.8 = (f32[4,64]{1,0:T(4,128)S(1)}, f32[4,64]{1,0:T(4,128)}, u32[]{:S(2)}) copy-start(f32[4,64]{1,0:T(4,128)} %param.31) | copy-start | bytes 3076
  19.4 63.1 %copy-start.6 = (f32[4,256]{1,0:T(4,128)S(1)}, f32[4,256]{1,0:T(4,128)}, u32[]{:S(2)}) copy-start(f32[4,256]{1,0:T(4,128)} %param.29) | copy-start | bytes 12292
  82.7 4.8 copy-start.2
  87.4 1.9 copy-start.10
  90.4 653.4 %reduce-scatter.2.cloned.1.call-start = ((), (), s32[]{:S(2)}) async-start(), calls=%async_computation.4 | async-start | bytes 6488064 | tf_op jit(solution)/shard_map/reduce_scatter | solution.py:156
  90.6 9.3 %copy-start.9 = (f32[256]{0:T(256)S(1)}, f32[256]{0:T(256)}, u32[]{:S(2)}) copy-start(f32[256]{0:T(256)} %param.30) | copy-start | bytes 3076
  90.6 9.8 %copy-start.13 = (bf16[8192,4]{0,1:T(4,128)(2,1)S(1)}, bf16[8192,4]{0,1:T(4,128)(2,1)}, u32[]{:S(2)}) copy-start(bf16[8192,4]{0,1:T(4,128)(2,1)} %param.28) | copy-start | bytes 196612
  90.6 9.8 %copy-start.16 = (f32[4]{0:T(128)S(1)}, f32[4]{0:T(128)}, u32[]{:S(2)}) copy-start(f32[4]{0:T(128)} %param.33) | copy-start | bytes 52
  218.0 306.0 %copy-start.3 = (f32[24,16,4,64]{3,2,1,0:T(4,128)S(1)}, f32[24,16,4,64]{3,2,1,0:T(4,128)}, u32[]{:S(2)}) copy-start(f32[24,16,4,64]{3,2,1,0:T(4,128)} %reshape_squeeze.3) | copy-start | bytes 1179652
  218.0 306.0 %copy-start.12 = (f32[4]{0:T(128)S(1)}, f32[4]{0:T(128)}, u32[]{:S(2)}) copy-start(f32[4]{0:T(128)} %param.35) | copy-start | bytes 52
  218.0 436.2 %copy-start.7 = (f32[256]{0:T(256)S(1)}, f32[256]{0:T(256)}, u32[]{:S(2)}) copy-start(f32[256]{0:T(256)} %param.36) | copy-start | bytes 3076
  654.2 89.6 %copy-start.1 = (bf16[8192,64]{0,1:T(8,128)(2,1)S(1)}, bf16[8192,64]{0,1:T(8,128)(2,1)}, u32[]{:S(2)}) copy-start(bf16[8192,64]{0,1:T(8,128)(2,1)} %param.27) | copy-start | bytes 3145732
Sparse Core Ops, SparseCore 0:
  9.5 57.0 all-gather.6
  68.3 82.6 all-gather.4
  153.2 53.9 all-gather.8
  661.1 82.6 reduce-scatter.1
where the time goes:
time: 753 us; the launch traced here: 750 us
  matrix products  199 us (26%)
  blocking collectives  177 us (24%)
  waiting for transfers between devices  155 us (21%)
  other arithmetic  131 us (17%)
  local copies, waits for them, and re-layouts  75.8 us (10%)
  between operations  13.5 us (2%)
    dot_general x24, matrix products, advance(): jnp.einsum('bhpn,bn->bhp', state_now, output_now, precision=lax.Precision...  172 us
    psum x1, blocking collectives, body(): summed = lax.psum(slots, 'head')  127 us
    add x24, other arithmetic, advance(): decay_now[:, :, None, None] * state_now  95.7 us
    reduce_scatter x1, waiting for transfers between devices, body(): lax.psum_scatter(output_terms.astype(jnp.bfloat16), 'head', scatter_dimen...  82.8 us
    all_gather x1, waiting for transfers between devices, body(): lax.all_gather(recurrent_state.astype(jnp.bfloat16), 'dom', axis=0, tiled...  40.1 us
    all_gather x1, waiting for transfers between devices, body(): lax.all_gather(mixing_act.astype(jnp.bfloat16), 'head', axis=2, tiled=True)  30.9 us
    all_gather x1, blocking collectives, body(): lax.all_gather(input_gain.astype(jnp.bfloat16), 'head', axis=0, tiled=True)  25.8 us
    squeeze x24, local copies, waits for them, and re-layouts, body(): lax.scan(advance, start_state, (value_act, input_mix, output_mix, step_si...  17.2 us
  transfers between devices with their start and end apart: 4, of which 3 were waited for; matrix products, arithmetic and copies ran while one was open for 10% of the time, Pallas kernels for 0%

commit v1 on v0

--- a/solution.py
+++ b/solution.py
@@ -6,6 +6,14 @@
 HEADS = 128
 GROUPS = 4
 P_SIZE = 64
+
+
+def gather_from_all(array, axis, dim):
+    size = lax.axis_size(axis)
+    repeats = [size if d == dim else 1 for d in range(array.ndim)]
+    return lax.all_to_all(
+        jnp.tile(array, repeats), axis, split_axis=dim, concat_axis=dim, tiled=True
+    )
 
 
 def causal_conv(previous, current, kernel, shift_bias):
@@ -62,9 +70,7 @@
     head_index = lax.axis_index("head")
     gathered, full_gain = (
         lax.all_gather(tokens, "head", axis=2, tiled=True),
-        lax.all_gather(input_gain.astype(jnp.bfloat16), "head", axis=0, tiled=True).astype(
-            input_gain.dtype
-        ),
+        gather_from_all(input_gain.astype(jnp.bfloat16), "head", 0).astype(input_gain.dtype),
     )
     flat_tokens = gathered.astype(jnp.float32).reshape(row_count, -1)
     normed = (

time: 753 us -> 752 us (level)
  blocking collectives: 177 us -> 151 us
  waiting for transfers between devices: 155 us -> 169 us
  starting transfers between devices: 0.31 us -> 8.75 us
    all_gather x1 -> x0, blocking collectives: 25.8 us -> none  [body(): lax.all_gather(input_gain.astype(jnp.bfloat16), 'head', axis=0, tiled=True)]
    all_gather x1, waiting for transfers between devices: 40.1 us -> 54.1 us  [body(): lax.all_gather(recurrent_state.astype(jnp.bfloat16), 'dom', axis=0, tiled...]
    all_to_all x0 -> x1, starting transfers between devices: none -> 8.42 us  [gather_from_all(): lax.all_to_all(jnp.tile(array, repeats), axis, split_axis=dim, concat_axi...]
  transfers between devices with their start and end apart: 4 -> 5, of which waited for: 3 -> 3; matrix products, arithmetic and copies ran while one was open for 10% -> 11% of each run, Pallas kernels for 0% -> 0%
where the time goes in v1:
time: 752 us; the launch traced here: 749 us
  matrix products  200 us (27%)
  waiting for transfers between devices  169 us (22%)
  blocking collectives  151 us (20%)
  other arithmetic  129 us (17%)
  local copies, waits for them, and re-layouts  77.5 us (10%)
  between operations  13.5 us (2%)
  starting transfers between devices  8.75 us (1%)
    dot_general x24, matrix products, advance(): jnp.einsum('bhpn,bn->bhp', state_now, output_now, precision=lax.Precision...  172 us
    psum x1, blocking collectives, body(): summed = lax.psum(slots, 'head')  127 us
    add x24, other arithmetic, advance(): decay_now[:, :, None, None] * state_now  93.8 us
    reduce_scatter x1, waiting for transfers between devices, body(): lax.psum_scatter(output_terms.astype(jnp.bfloat16), 'head', scatter_dimen...  82.8 us
    all_gather x1, waiting for transfers between devices, body(): lax.all_gather(recurrent_state.astype(jnp.bfloat16), 'dom', axis=0, tiled...  54.1 us
    all_gather x1, waiting for transfers between devices, body(): lax.all_gather(mixing_act.astype(jnp.bfloat16), 'head', axis=2, tiled=True)  31.1 us
    squeeze x24, local copies, waits for them, and re-layouts, body(): lax.scan(advance, start_state, (value_act, input_mix, output_mix, step_si...  17.2 us
    dynamic_update_slice x24, local copies, waits for them, and re-layouts, body(): lax.scan(advance, start_state, (value_act, input_mix, output_mix, step_si...  15.1 us
  transfers between devices with their start and end apart: 5, of which 3 were waited for; matrix products, arithmetic and copies ran while one was open for 11% of the time, Pallas kernels for 0%

profile of v1, /device:TPU:0, one launch (start us, length us, event | category | flops | bytes accessed | tf_op | source)
XLA Modules:
  0.0 748.7 jit_solution(8467269915737256986)
XLA Ops:
  13.1 8.4 %all-to-all-start = ((bf16[32,2,128]{2,1,0:T(2,128)(2,1)}), bf16[32,2,128]{2,1,0:T(2,128)(2,1)S(1)}, u32[]{:S(2)}, u32[]{:S(2)}) async-start(bf16[32,2,128]{2,1,0:T(2,128)(2,1)} %reshape.158), calls=%async_computation | async-start | bytes 32768 | tf_op jit(solution)/shard_map/all_to_all | solution.py:14
  21.7 12.3 %all_gather.17 = bf16[64,3,256]{2,0,1:T(8,128)(2,1)S(1)} all-gather(bf16[16,3,256]{2,0,1:T(8,128)(2,1)S(1)} %convert_element_type.60), channel_id=1, replica_groups=mesh['dom'=4,'head'=32] {'dom'}, dimensions={0}, use_global_device_ids=true | all-gather | bytes 122880 | tf_op jit(solution)/shard_map/all_gather | solution.py:105
  34.0 11.9 %all_gather.18 = bf16[64,3,64]{2,0,1:T(8,128)(2,1)S(1)} all-gather(bf16[16,3,64]{2,0,1:T(8,128)(2,1)S(1)} %convert_element_type.62), channel_id=1, replica_groups=mesh['dom'=4,'head'=32] {'dom'}, dimensions={0}, use_global_device_ids=true | all-gather | bytes 30720 | tf_op jit(solution)/shard_map/all_gather | solution.py:108
  47.5 8.0 %copy.52 = bf16[1024,8,2,256]{3,1,2,0:T(8,128)(2,1)} copy(bf16[1024,8,2,256]{3,2,1,0:T(2,128)(2,1)} %bitcast.82) | data formatting | bytes 16777216
  55.6 12.1 %copy.43 = bf16[512,8192]{1,0:T(8,128)(2,1)} copy(bf16[512,8192]{0,1:T(8,128)(2,1)} %bitcast.81) | data formatting | bytes 16777216 | tf_op jit(solution)/shard_map/dot_general | solution.py:81
  75.6 9.1 %fusion.5 = f32[24,16,2,256]{3,1,2,0:T(8,128)S(1)} fusion(bf16[2,256,8192,1]{2,1,0,3:T(8,128)(2,1)} %bitcast.83, bf16[24,16,8192]{2,1,0:T(8,128)(2,1)} %all-gather.6.cloned.1.call-done, f32[8192]{0:T(1024)S(1)} %bitcast.86, f32[24,16]{1,0:T(8,128)S(1)} %add_rsqrt_fusion.1), kind=kOutput, calls=%fused_computation.18 | convolution fusion | flops 3233808384 | bytes 15500800 | tf_op jit(solution)/shard_map/dot_general | solution.py:81
  86.6 10.3 %multiply_exponential_fusion = (f32[24,16,4]{1,2,0:T(4,128)S(1)}, f32[24,16,4]{1,2,0:T(4,128)S(1)}) fusion(f32[4]{0:T(128)S(1)} %exp.23, f32[4]{0:T(128)S(1)} %copy-done.16, bf16[8192,4]{0,1:T(4,128)(2,1)S(1)} %copy-done.13, bf16[24,16,8192]{2,1,0:T(8,128)(2,1)} %all-gather.6.cloned.1.call-done, f32[8192]{0:T(1024)S(1)} %bitcast.87, ...), kind=kOutput, calls=%fused_computation.69 | convolution fusion | flops 37762560 | bytes 6403616 | tf_op jit(solution)/shard_map/dot_general | solution.py:89
  96.9 54.1 %all-gather.4.cloned.1.call-done = bf16[64,4,64,256]{3,2,1,0:T(8,128)(2,1)} async-done(((bf16[16,4,64,256]{3,2,1,0:T(8,128)(2,1)}), bf16[64,4,64,256]{3,2,1,0:T(8,128)(2,1)}) %all-gather.4.cloned.1.call-update) | async-done | bytes 8388624 | tf_op jit(solution)/shard_map/all_gather | solution.py:102
  151.0 11.3 %convert_element_type.54 = f32[64,4,64,256]{3,2,1,0:T(8,128)} convert(bf16[64,4,64,256]{3,2,1,0:T(8,128)(2,1)} %all-gather.4.cloned.1.call-done) | non-fusion elementwise | flops 4194304 | bytes 25165824 | tf_op jit(solution)/shard_map/convert_element_type | solution.py:102
  162.3 8.8 %gather_fusion = f32[16,4,64,256]{3,2,1,0:T(8,128)} fusion(f32[64,4,64,256]{3,2,1,0:T(8,128)} %convert_element_type.54, s32[1024]{0:T(1024)S(1)} %pad_clamp_fusion), kind=kCustom, calls=%fused_computation | custom fusion | bytes 8388672 | tf_op jit(solution)/shard_map/jit(_take)/gather | solution.py:34
  176.2 31.1 %all-gather.8.cloned.1.call-done = bf16[24,16,2048]{0,1,2:T(8,128)(2,1)} async-done(((bf16[24,16,64]{0,1,2:T(8,128)(2,1)}), bf16[24,16,2048]{0,1,2:T(8,128)(2,1)}) %all-gather.8.cloned.1.call-update) | async-done | bytes 1572880 | tf_op jit(solution)/shard_map/all_gather | solution.py:118
  218.1 304.3 %while.12 = (s32[]{:T(128)}, f32[16,4,64,256]{3,2,1,0:T(8,128)}, f32[24,16,4,64]{3,2,1,0:T(4,128)}, f32[24,16,4]{1,2,0:T(4,128)S(1)}, f32[24,16,4]{1,2,0:T(4,128...) while((s32[]{:T(128)}, f32[16,4,64,256]{3,2,1,0:T(8,128)}, ...), condition=%wide.region_2.3_spmd, body=%wide.region_1.2_spmd.sunk | while | flops 15732738 | bytes 12798585 | solution.py:142
  223.0 7.2 fusion.55
  235.7 7.2 fusion.55
  248.4 7.2 fusion.55
  261.0 7.2 fusion.55
  273.7 7.2 fusion.55
  286.4 7.2 fusion.55
  299.1 7.2 fusion.55
  324.4 7.2 fusion.55
  451.2 7.2 fusion.55
  476.6 7.2 fusion.55
  525.0 126.5 %psum.7 = f32[24,16,4]{1,2,0:T(4,128)S(1)} all-reduce(f32[24,16,4]{1,2,0:T(4,128)S(1)} %broadcast_select_fusion), channel_id=1, replica_groups=mesh['dom'=4,'head'=32] {'head'}, use_global_device_ids=true, to_apply=%region_4.5 | all-reduce | flops 1536 | bytes 12288 | tf_op jit(solution)/shard_map/psum | solution.py:152
  659.4 82.8 %reduce-scatter.2.cloned.1.call-done = bf16[24,16,256]{2,1,0:T(8,128)(2,1)} async-done(((bf16[24,16,8192]{2,1,0:T(8,128)(2,1)}), bf16[24,16,256]{2,1,0:T(8,128)(2,1)}) %reduce-scatter.2.cloned.1.call-update) | async-done | bytes 196624 | tf_op jit(solution)/shard_map/reduce_scatter | solution.py:162
  (294 shorter events, 276.6 us)
Async XLA Ops:
  6.5 65.5 %copy-start = (bf16[8192,64]{0,1:T(8,128)(2,1)S(1)}, bf16[8192,64]{0,1:T(8,128)(2,1)}, u32[]{:S(2)}) copy-start(bf16[8192,64]{0,1:T(8,128)(2,1)} %param.27) | copy-start | bytes 3145732
  6.5 4.7 copy-start.14
  6.5 15.1 %copy-start.4 = (f32[16,3,256]{2,0,1:T(8,128)S(1)}, f32[16,3,256]{2,0,1:T(8,128)}, u32[]{:S(2)}) copy-start(f32[16,3,256]{2,0,1:T(8,128)} %param.23) | copy-start | bytes 147460
  6.5 27.5 %copy-start.5 = (f32[16,3,64]{2,0,1:T(8,128)S(1)}, f32[16,3,64]{2,0,1:T(8,128)}, u32[]{:S(2)}) copy-start(f32[16,3,64]{2,0,1:T(8,128)} %param.24) | copy-start | bytes 36868
  6.5 39.5 %copy-start.11 = (s32[64]{0:T(128)S(1)}, s32[64]{0:T(128)}, u32[]{:S(2)}) copy-start(s32[64]{0:T(128)} %param.21) | copy-start | bytes 772
  6.5 40.8 %copy-start.8 = (f32[4,64]{1,0:T(4,128)S(1)}, f32[4,64]{1,0:T(4,128)}, u32[]{:S(2)}) copy-start(f32[4,64]{1,0:T(4,128)} %param.31) | copy-start | bytes 3076
  6.6 40.8 %copy-start.6 = (f32[4,256]{1,0:T(4,128)S(1)}, f32[4,256]{1,0:T(4,128)}, u32[]{:S(2)}) copy-start(f32[4,256]{1,0:T(4,128)} %param.29) | copy-start | bytes 12292
  6.6 61.2 %all-gather.6.cloned.1.call-start = ((), (), s32[]{:S(2)}) async-start(), calls=%async_computation.3 | async-start | bytes 6488064 | tf_op jit(solution)/shard_map/all_gather | solution.py:72
  7.3 143.7 %all-gather.4.cloned.1.call-start = ((), (), s32[]{:S(2)}) async-start(), calls=%async_computation.2 | async-start | bytes 10485760 | tf_op jit(solution)/shard_map/all_gather | solution.py:102
  13.1 54.5 %all-to-all-start = ((bf16[32,2,128]{2,1,0:T(2,128)(2,1)}), bf16[32,2,128]{2,1,0:T(2,128)(2,1)S(1)}, u32[]{:S(2)}, u32[]{:S(2)}) async-start(bf16[32,2,128]{2,1,0:T(2,128)(2,1)} %reshape.158), calls=%async_computation | async-start | bytes 32768 | tf_op jit(solution)/shard_map/all_to_all | solution.py:14
  21.6 185.7 %all-gather.8.cloned.1.call-start = ((), (), s32[]{:S(2)}) async-start(), calls=%async_computation.4 | async-start | bytes 8650752 | tf_op jit(solution)/shard_map/all_gather | solution.py:118
  55.6 12.1 %copy-start.15 = (f32[4]{0:T(128)S(1)}, f32[4]{0:T(128)}, u32[]{:S(2)}) copy-start(f32[4]{0:T(128)} %param.34) | copy-start | bytes 52
  67.8 4.6 copy-start.2
  72.4 1.9 copy-start.10
  75.4 666.8 %reduce-scatter.2.cloned.1.call-start = ((), (), s32[]{:S(2)}) async-start(), calls=%async_computation.5 | async-start | bytes 6488064 | tf_op jit(solution)/shard_map/reduce_scatter | solution.py:162
  75.6 10.5 %copy-start.9 = (f32[256]{0:T(256)S(1)}, f32[256]{0:T(256)}, u32[]{:S(2)}) copy-start(f32[256]{0:T(256)} %param.30) | copy-start | bytes 3076
  75.6 11.0 %copy-start.13 = (bf16[8192,4]{0,1:T(4,128)(2,1)S(1)}, bf16[8192,4]{0,1:T(4,128)(2,1)}, u32[]{:S(2)}) copy-start(bf16[8192,4]{0,1:T(4,128)(2,1)} %param.28) | copy-start | bytes 196612
  75.6 11.0 %copy-start.16 = (f32[4]{0:T(128)S(1)}, f32[4]{0:T(128)}, u32[]{:S(2)}) copy-start(f32[4]{0:T(128)} %param.33) | copy-start | bytes 52
  218.1 304.3 %copy-start.3 = (f32[24,16,4,64]{3,2,1,0:T(4,128)S(1)}, f32[24,16,4,64]{3,2,1,0:T(4,128)}, u32[]{:S(2)}) copy-start(f32[24,16,4,64]{3,2,1,0:T(4,128)} %reshape_squeeze.3) | copy-start | bytes 1179652
  218.1 304.3 %copy-start.12 = (f32[4]{0:T(128)S(1)}, f32[4]{0:T(128)}, u32[]{:S(2)}) copy-start(f32[4]{0:T(128)} %param.35) | copy-start | bytes 52
  218.1 434.5 %copy-start.7 = (f32[256]{0:T(256)S(1)}, f32[256]{0:T(256)}, u32[]{:S(2)}) copy-start(f32[256]{0:T(256)} %param.36) | copy-start | bytes 3076
  652.6 89.6 %copy-start.1 = (bf16[8192,64]{0,1:T(8,128)(2,1)S(1)}, bf16[8192,64]{0,1:T(8,128)(2,1)}, u32[]{:S(2)}) copy-start(bf16[8192,64]{0,1:T(8,128)(2,1)} %param.27) | copy-start | bytes 3145732
Sparse Core Ops, SparseCore 0:
  9.6 57.0 all-gather.5
  68.4 82.5 all-gather.3
  153.3 53.9 all-gather.7
  659.5 82.6 reduce-scatter.1
